TPU v7x, 512 devices: a whole 4x8x8 slice. The times are simulated.
512 devices in a mesh: slab: 64 (over x, z, core), dp: 8 (over y).
Axes of the slice: x: 4, y: 8, z: 8, core: 2. Of those that a mesh axis runs over, the one named last changes fastest.
Arguments:
- point_feats: float32 [8, 32768, 128], P('dp', 'slab'), may hold values from -6 to 6
- owner_slab: int32 [8, 32768, 1], P('dp', 'slab'), may hold values from 0 to 63; in each aligned block of 512 rows (0 to 511, 512 to 1023, ..., all dimensions but the last counted through in order) at most 16 rows name the same one
- block_slot: int32 [8, 32768], P('dp', 'slab'), may hold values from 0 to 1
- voxel_index: int32 [8, 32768], P('dp', 'slab'), may hold values from 0 to 511
- boundary: int32 [8, 64, 2, 1], P('dp', 'slab'), may hold values from 0 to 1, as said below
- neighbours: int32 [8, 128, 27], P('dp', 'slab'), may hold values from 0 to 4, as said below
- weight_taps: float32 [27, 128, 128], replicated, may hold values from -0.109375 to 0.109375
- cotangent: float32 [8, 65536, 128], P('dp', 'slab'), may hold values from -6 to 6
Outputs:
- activated: float32 [8, 65536, 128], P('dp', 'slab')
- point_grads: float32 [8, 32768, 128], P('dp', 'slab')
- weight_grads: float32 [3456, 128], P('slab')
Inputs may be any that keep to these rules, and one draw needn't show every extreme that they name: `owner_slab`: among the points of one device, no slab is named by more than 16 points, and exactly 16 in some device. `boundary`: each list of one slab holds 1 different block slots. `neighbours`: entry 13 of a block's row is the block's own slot. Entries 0 to 8 name a block of the slab (below 2), one of the 1 block from the slab before (2 to 2), or the zero block 4; entries 18 to 26 a block of the slab, one of the 1 block from the slab after, or the zero block; the others a block of the slab or the zero block.
All inputs are finite; a program needn't handle non-finite values.
Results may differ from a plain program's by a relative error of at most 0.0003.
Values sent between devices are 32-bit elements; how exact they have to be, the bound alone decides.
A program may use at most 64 MiB of HBM per device.

v0:
```python
import math
import jax
import jax.numpy as jnp
import numpy as np
from jax import lax
from jax.sharding import PartitionSpec as P

C = 128
E = 8
NB = 2
NH = 1
P_DEV = 512
VOX = 512
highest = lax.Precision.HIGHEST


def padded_2(value, sides, width):
    for axis, dim in sides:
        size, length = (lax.axis_size(axis), value.shape[dim])
        up = [(i, (i + 1) % size) for i in range(size)]
        down = [(j, i) for i, j in up]
        last = lax.slice_in_dim(value, length - width, length, axis=dim)
        leading = lax.slice_in_dim(value, 0, width, axis=dim)
        before = lax.ppermute(last, axis, up)
        after = lax.ppermute(leading, axis, down)
        value = jnp.concatenate([before, value, after], axis=dim)
    return value


def grid_tables():
    padded_edge = E + 2
    position = np.arange(padded_edge)
    section = np.where(position == 0, 0, np.where(position == padded_edge - 1, 2, 1))
    within = np.where(position == 0, E - 1, np.where(position == padded_edge - 1, 0, position - 1))
    grid_x, grid_y, grid_z = np.meshgrid(position, position, position, indexing="ij")
    tap_table = section[grid_x] * 9 + section[grid_y] * 3 + section[grid_z]
    voxel_table = within[grid_x] * E * E + within[grid_y] * E + within[grid_z]
    return (
        jnp.asarray(tap_table.reshape(-1), jnp.int32),
        jnp.asarray(voxel_table.reshape(-1), jnp.int32),
    )


def column_block(padded, tap_x):
    parts_list = [
        padded[:, tap_x : tap_x + E, tap_y : tap_y + E, tap_z : tap_z + E]
        for tap_y in range(3)
        for tap_z in range(3)
    ]
    return jnp.concatenate(parts_list, axis=-1).reshape(NB * VOX, 9 * C)


def per_device(
    point_feats, owner_slab, block_slot, voxel_index, boundary, neighbours, weight_taps, cotangent
):
    slabs = lax.axis_size("slab")
    windows = lax.axis_size("dp")
    capacity = 2 * P_DEV // slabs
    features = point_feats[0]
    target = owner_slab[0, :, 0]
    onehot = (target[:, None] == jnp.arange(slabs)[None, :]).astype(jnp.int32)
    ranks = jnp.sum((jnp.cumsum(onehot, axis=0) - onehot) * onehot, axis=1)
    placement = target * capacity + ranks
    send_rows = jnp.zeros((slabs * capacity, C), jnp.float32).at[placement].set(features)
    send_ids = (
        jnp.full((slabs * capacity,), -1, jnp.int32)
        .at[placement]
        .set(block_slot[0] * VOX + voxel_index[0])
    )
    recv_rows, recv_ids = (
        lax.all_to_all(
            send_rows.reshape(slabs, capacity, C), "slab", split_axis=0, concat_axis=0, tiled=True
        ),
        lax.all_to_all(
            send_ids.reshape(slabs, capacity), "slab", split_axis=0, concat_axis=0, tiled=True
        ),
    )
    flat_ids = recv_ids.reshape(-1)
    target_rows = jnp.where(flat_ids < 0, NB * VOX, flat_ids)
    voxel_feats = (
        jnp.zeros((NB * VOX + 1, C), jnp.float32)
        .at[target_rows]
        .add(recv_rows.reshape(-1, C))[: NB * VOX]
    )
    blocks = voxel_feats.reshape(NB, VOX, C)
    lend_left = boundary[0, 0, 0]
    lend_right = boundary[0, 0, 1]
    sent_left = blocks[lend_left]
    sent_right = blocks[lend_right]
    arrived = padded_2(jnp.stack((sent_left, sent_right)), (("slab", 0),), 1)
    from_left = arrived[0]
    from_right = arrived[3]
    slots_all = NB + 2 * NH + 1
    visible = jnp.concatenate(
        [blocks, from_left, from_right, jnp.zeros((1, VOX, C), jnp.float32)], axis=0
    )
    flat_visible = visible.reshape(slots_all * VOX, C)
    tap_table, voxel_table = grid_tables()
    gather_rows = neighbours[0][:, tap_table] * VOX + voxel_table[None, :]
    padded = flat_visible[gather_rows].reshape(NB, E + 2, E + 2, E + 2, C)
    pre_act = jnp.zeros((NB * VOX, C), jnp.float32)
    for tap_x in range(3):
        columns = column_block(padded, tap_x)
        group_weight = weight_taps[tap_x * 9 : tap_x * 9 + 9].reshape(9 * C, C)
        pre_act = pre_act + jnp.dot(
            columns, group_weight, precision=highest, preferred_element_type=jnp.float32
        )
    gate_value = jax.nn.sigmoid(pre_act)
    activated = pre_act * gate_value
    grad_pre = cotangent[0] * gate_value * (1.0 + pre_act * (1.0 - gate_value))
    pieces = []
    back_groups = []
    for tap_x in range(3):
        columns = column_block(padded, tap_x)
        pieces.append(
            lax.dot_general(
                columns,
                grad_pre,
                (((0,), (0,)), ((), ())),
                precision=highest,
                preferred_element_type=jnp.float32,
            )
        )
        group_back = weight_taps[tap_x * 9 : tap_x * 9 + 9].transpose(2, 0, 1).reshape(C, 9 * C)
        back_groups.append(
            jnp.dot(
                grad_pre, group_back, precision=highest, preferred_element_type=jnp.float32
            ).reshape(NB, E, E, E, 9, C)
        )
    weight_term = jnp.concatenate(pieces, axis=0)
    grad_padded = jnp.zeros((NB, E + 2, E + 2, E + 2, C), jnp.float32)
    for tap_x in range(3):
        for tap_y in range(3):
            for tap_z in range(3):
                shifted = back_groups[tap_x][:, :, :, :, tap_y * 3 + tap_z]
                grad_padded = grad_padded + jnp.pad(
                    shifted,
                    ((0, 0), (tap_x, 2 - tap_x), (tap_y, 2 - tap_y), (tap_z, 2 - tap_z), (0, 0)),
                )
    grad_visible = (
        jnp.zeros((slots_all * VOX, C), jnp.float32)
        .at[gather_rows.reshape(-1)]
        .add(grad_padded.reshape(-1, C))
    )
    grad_visible = grad_visible.reshape(slots_all, VOX, C)
    left_grads = grad_visible[NB : NB + NH]
    right_grads = grad_visible[NB + NH : NB + 2 * NH]
    returned = padded_2(jnp.stack((left_grads, right_grads)), (("slab", 0),), 1)
    for_lent_left = returned[0]
    for_lent_right = returned[3]
    grad_blocks = (
        grad_visible[:NB].at[lend_left].add(for_lent_left).at[lend_right].add(for_lent_right)
    )
    grad_flat = jnp.concatenate(
        [grad_blocks.reshape(NB * VOX, C), jnp.zeros((1, C), jnp.float32)], axis=0
    )
    back_points = grad_flat[target_rows].reshape(slabs, capacity, C)
    came_back = lax.all_to_all(back_points, "slab", split_axis=0, concat_axis=0, tiled=True)
    point_grads = came_back.reshape(slabs * capacity, C)[placement]
    share = lax.psum_scatter(weight_term, "slab", scatter_dimension=0, tiled=True)
    total = lax.psum(share, "dp")
    scale = 1.0 / math.sqrt(windows * slabs * NB * VOX)
    return (activated[None], point_grads[None], total * scale)


def solution(mesh):
    return jax.shard_map(
        per_device,
        mesh=mesh,
        in_specs=(
            P("dp", "slab", None),
            P("dp", "slab", None),
            P("dp", "slab"),
            P("dp", "slab"),
            P("dp", "slab", None, None),
            P("dp", "slab", None),
            P(),
            P("dp", "slab", None),
        ),
        out_specs=(P("dp", "slab", None), P("dp", "slab", None), P("slab", None)),
        check_vma=False,
    )
```

profile of v0, /device:TPU:4, one launch (start us, length us, event | category | flops | bytes accessed | tf_op | source)
XLA Modules:
  0.0 403.9 jit_solution(14868015423676881469)
XLA Ops:
  8.2 13.9 %all-to-all-start = ((s32[64,1,16]{2,1,0:T(1,128)}), s32[64,1,16]{2,1,0:T(1,128)S(1)}, u32[]{:S(2)}, u32[]{:S(2)}) async-start(s32[64,1,16]{2,1,0:T(1,128)} %bitcast.7), calls=%async_computation | async-start | bytes 65536 | tf_op jit(solution)/shard_map/all_to_all | solution.py:74
  34.9 10.3 %all-to-all-start.1 = ((f32[64,16,128]{2,1,0:T(8,128)}), f32[64,16,128]{2,1,0:T(8,128)S(1)}, u32[]{:S(2)}, u32[]{:S(2)}) async-start(f32[64,16,128]{2,1,0:T(8,128)} %bitcast.10), calls=%async_computation.1 | async-start | bytes 1048576 | tf_op jit(solution)/shard_map/all_to_all | solution.py:71
  46.6 2.9 gather_fusion
  49.8 12.1 %all-to-all-done.1 = f32[64,16,128]{2,1,0:T(8,128)S(1)} async-done(((f32[64,16,128]{2,1,0:T(8,128)}), f32[64,16,128]{2,1,0:T(8,128)S(1)}, u32[]{:S(2)}, u32[]{:S(2)}) %all-to-all-start.1) | async-done | bytes 524320 | tf_op jit(solution)/shard_map/all_to_all | solution.py:71
  61.9 6.2 %scatter_custom_fusion.2 = f32[1025,128]{1,0:T(8,128)S(1)} fusion(s32[1024]{0:T(1024)S(1)} %bitcast.239, f32[1024,128]{1,0:T(8,128)S(1)} %bitcast.232, f32[]{:T(128)} %constant.74.clone.1), kind=kCustom, calls=%fused_computation.81 | custom fusion | flops 131072 | bytes 524804 | tf_op jit(solution)/shard_map/scatter-add | solution.py:83
  70.6 5.2 %collective-permute-start.1 = (f32[1,1,512,128]{3,2,1,0:T(8,128)S(1)}, f32[1,1,512,128]{3,2,1,0:T(8,128)S(1)}, u32[]{:S(2)}, u32[]{:S(2)}) collective-permute-start(f32[1,1,512,128]{3,2,1,0:T(8,128)S(1)} %get-tuple-element.113), channel_id=1, source_target_pairs={{8,0},{16,8},{24,16},{32,24},{40,32},{48,40},{56,48},{64,56},{72,6... | collective-permute-start | bytes 786440 | tf_op jit(solution)/shard_map/ppermute | solution.py:25
  79.9 5.8 %gather_fusion.1 = f32[2000,128]{1,0:T(8,128)S(1)} fusion(f32[2560,128]{1,0:T(8,128)S(1)} %bitcast.213, s32[2048]{0:T(1024)S(1)} %pad_clamp_fusion), kind=kCustom, calls=%fused_computation.1 | custom fusion | bytes 2056000 | tf_op jit(solution)/shard_map/gather | solution.py:100
  88.1 4.1 %fusion.28 = f32[1024,128]{1,0:T(8,128)S(1)} fusion(f32[1024,1152]{1,0:T(8,128)S(1)} %bitcast.221, f32[1152,128]{1,0:T(8,128)S(1)} %bitcast.230), kind=kOutput, calls=%fused_computation.130 | convolution fusion | flops 1811939328 | bytes 5832704 | tf_op jit(solution)/shard_map/dot_general | solution.py:105
  92.2 4.1 %convolution_add_fusion.1 = f32[1024,128]{1,0:T(8,128)S(1)} fusion(f32[1024,128]{1,0:T(8,128)S(1)} %fusion.28, f32[1024,1152]{1,0:T(8,128)S(1)} %bitcast.219, f32[1152,128]{1,0:T(8,128)S(1)} %bitcast.229), kind=kOutput, calls=%fused_computation.12 | convolution fusion | flops 1812070400 | bytes 6356992 | tf_op jit(solution)/shard_map/dot_general | solution.py:105
  96.3 5.4 %fusion.9 = (f32[1024,128]{1,0:T(8,128)S(1)}, f32[1,1024,128]{2,1,0:T(8,128)}) fusion(f32[1,1024,128]{2,1,0:T(8,128)S(1)} %copy-done.7, f32[1024,128]{1,0:T(8,128)S(1)} %convolution_add_fusion.1, f32[1024,1152]{1,0:T(8,128)S(1)} %bitcast.217, f32[1152,128]{1,0:T(8,128)S(1)} %bitcast.228), kind=kOutput, calls=%fused_computation.76 | convolution fusion | flops 1813250048 | bytes 7405568 | tf_op jit(solution)/shard_map/dot_general | solution.py:105
  101.7 7.7 %fusion.29 = f32[1152,128]{1,0:T(8,128)S(1)} fusion(f32[1024,1152]{1,0:T(8,128)S(1)} %bitcast.222, f32[1024,128]{1,0:T(8,128)S(1)} %get-tuple-element.110), kind=kOutput, calls=%fused_computation.131 | convolution fusion | flops 1811939328 | bytes 5832704 | tf_op jit(solution)/shard_map/dot_general | solution.py:116
  109.4 8.7 %fusion.30 = f32[1152,128]{1,0:T(8,128)} fusion(f32[1024,1152]{1,0:T(8,128)S(1)} %bitcast.220, f32[1024,128]{1,0:T(8,128)S(1)} %get-tuple-element.110), kind=kOutput, calls=%fused_computation.132 | convolution fusion | flops 1811939328 | bytes 5832704 | tf_op jit(solution)/shard_map/dot_general | solution.py:116
  118.2 8.6 %fusion.31 = f32[1152,128]{1,0:T(8,128)} fusion(f32[1024,1152]{1,0:T(8,128)S(1)} %bitcast.218, f32[1024,128]{1,0:T(8,128)S(1)} %get-tuple-element.110), kind=kOutput, calls=%fused_computation.133 | convolution fusion | flops 1811939328 | bytes 5832704 | tf_op jit(solution)/shard_map/dot_general | solution.py:116
  126.7 4.2 %fusion.5 = f32[2,8,8,8,9,128]{5,3,2,1,0,4:T(8,128)S(1)} fusion(f32[2,8,8,8,128,1]{4,3,2,1,0,5:T(8,128)S(1)} %bitcast.214, f32[27,128,128]{2,1,0:T(8,128)S(1)} %copy-done.2), kind=kOutput, calls=%fused_computation.17 | convolution fusion | flops 1811939328 | bytes 5832704 | tf_op jit(solution)/shard_map/dot_general | solution.py:126
  131.0 3.8 fusion.3
  134.8 4.0 fusion.7
  141.2 2.9 pad_add_fusion
  145.2 12.2 %scatter_custom_fusion.3 = f32[2560,128]{1,0:T(8,128)S(1)} fusion(s32[2000]{0:T(1024)S(1)} %bitcast.244, f32[2000,128]{1,0:T(8,128)} %reshape.431, f32[]{:T(128)} %constant.74.clone.1), kind=kCustom, calls=%fused_computation.13 | custom fusion | flops 256000 | bytes 1311232 | tf_op jit(solution)/shard_map/scatter-add | solution.py:143
  159.4 5.9 %collective-permute-start.3 = (f32[1,1,512,128]{3,2,1,0:T(8,128)S(1)}, f32[1,1,512,128]{3,2,1,0:T(8,128)S(1)}, u32[]{:S(2)}, u32[]{:S(2)}) collective-permute-start(f32[1,1,512,128]{3,2,1,0:T(8,128)S(1)} %get-tuple-element.108), channel_id=1, source_target_pairs={{8,0},{16,8},{24,16},{32,24},{40,32},{48,40},{56,48},{64,56},{72,6... | collective-permute-start | bytes 786440 | tf_op jit(solution)/shard_map/ppermute | solution.py:25
  169.9 4.0 gather_fusion.2
  174.0 10.4 %all-to-all-start.2 = ((f32[64,16,128]{2,1,0:T(8,128)}), f32[64,16,128]{2,1,0:T(8,128)S(1)}, u32[]{:S(2)}, u32[]{:S(2)}) async-start(f32[64,16,128]{2,1,0:T(8,128)} %bitcast.231), calls=%async_computation.2 | async-start | bytes 1048576 | tf_op jit(solution)/shard_map/all_to_all | solution.py:158
  184.3 123.3 %fusion = f32[64,128]{1,0:T(8,128)S(1)} fusion(f32[3456,128]{1,0:T(8,128)S(1)} %pad_maximum_fusion), kind=kCustom, calls=%all-reduce-scatter | all-reduce-scatter fusion | flops 524289 | bytes 1804288
  309.5 4.5 %collective-permute-start.11 = (f32[64,128]{1,0:T(8,128)S(1)}, f32[64,128]{1,0:T(8,128)S(1)}, u32[]{:S(2)}, u32[]{:S(2)}) collective-permute-start(f32[64,128]{1,0:T(8,128)S(1)} %fusion), channel_id=1, source_target_pairs={{0,64},{8,72},{16,80},{24,88},{32,96},{40,104},{48,112},{56,120},{... | collective-permute-start | bytes 98312
  314.0 8.4 %collective-permute-start.12 = (f32[64,128]{1,0:T(8,128)S(1)}, f32[64,128]{1,0:T(8,128)S(1)}, u32[]{:S(2)}, u32[]{:S(2)}) collective-permute-start(f32[64,128]{1,0:T(8,128)S(1)} %fusion), channel_id=1, source_target_pairs={{0,72},{8,80},{16,88},{24,96},{32,104},{40,112},{48,120},{56,128},... | collective-permute-start | bytes 98312
  324.5 10.3 %collective-permute-start.13 = (f32[54,128]{1,0:T(8,128)S(1)}, f32[54,128]{1,0:T(8,128)S(1)}, u32[]{:S(2)}, u32[]{:S(2)}) collective-permute-start(f32[54,128]{1,0:T(8,128)S(1)} %slice.419), channel_id=1, source_target_pairs={{0,80},{8,88},{16,96},{24,104},{32,112},{40,120},{48,128},{56,136}... | collective-permute-start | bytes 82952
  336.3 7.7 %collective-permute-start.5 = (f32[64,128]{1,0:T(8,128)S(1)}, f32[64,128]{1,0:T(8,128)S(1)}, u32[]{:S(2)}, u32[]{:S(2)}) collective-permute-start(f32[64,128]{1,0:T(8,128)S(1)} %fusion), channel_id=1, source_target_pairs={{0,16},{8,24},{16,32},{24,40},{32,48},{40,56},{48,64},{56,72},{64,... | collective-permute-start | bytes 98312
  344.1 9.3 %collective-permute-start.6 = (f32[64,128]{1,0:T(8,128)S(1)}, f32[64,128]{1,0:T(8,128)S(1)}, u32[]{:S(2)}, u32[]{:S(2)}) collective-permute-start(f32[64,128]{1,0:T(8,128)S(1)} %fusion), channel_id=1, source_target_pairs={{0,24},{8,32},{16,40},{24,48},{32,56},{40,64},{48,72},{56,80},{64,... | collective-permute-start | bytes 98312
  353.4 3.1 collective-permute-start.7
  358.4 3.1 collective-permute-start.9
  363.5 2.8 collective-permute-done.8
  366.3 2.8 collective-permute-done.9
  370.8 30.4 %psum.7 = f32[54,128]{1,0:T(8,128)S(1)} all-reduce(f32[54,128]{1,0:T(8,128)S(1)} %constant_dynamic-slice_fusion), channel_id=1, replica_groups=mesh['slab'=64,'dp'=8] {'dp'}, use_global_device_ids=true, to_apply=%region_10.11 | all-reduce | flops 6912 | bytes 55296 | tf_op jit(solution)/shard_map/psum | solution.py:161
  (99 shorter events, 49.4 us)
Async XLA Ops:
  0.6 31.6 %copy-start = (f32[1,512,128]{2,1,0:T(8,128)S(1)}, f32[1,512,128]{2,1,0:T(8,128)}, u32[]{:S(2)}) copy-start(f32[1,512,128]{2,1,0:T(8,128)} %param.14) | copy-start | bytes 786436
  0.6 45.9 %copy-start.9 = (s32[1000]{0:T(1024)S(1)}, s32[1000]{0:T(1024)}, u32[]{:S(2)}) copy-start(s32[1000]{0:T(1024)} %constant.196) | copy-start | bytes 12004
  0.7 49.0 %copy-start.8 = (s32[1000]{0:T(1024)S(1)}, s32[1000]{0:T(1024)}, u32[]{:S(2)}) copy-start(s32[1000]{0:T(1024)} %constant.90.clone) | copy-start | bytes 12004
  8.2 26.6 %all-to-all-start = ((s32[64,1,16]{2,1,0:T(1,128)}), s32[64,1,16]{2,1,0:T(1,128)S(1)}, u32[]{:S(2)}, u32[]{:S(2)}) async-start(s32[64,1,16]{2,1,0:T(1,128)} %bitcast.7), calls=%async_computation | async-start | bytes 65536 | tf_op jit(solution)/shard_map/all_to_all | solution.py:74
  34.9 27.0 %all-to-all-start.1 = ((f32[64,16,128]{2,1,0:T(8,128)}), f32[64,16,128]{2,1,0:T(8,128)S(1)}, u32[]{:S(2)}, u32[]{:S(2)}) async-start(f32[64,16,128]{2,1,0:T(8,128)} %bitcast.10), calls=%async_computation.1 | async-start | bytes 1048576 | tf_op jit(solution)/shard_map/all_to_all | solution.py:71
  68.2 9.8 %collective-permute-start = (f32[1,1,512,128]{3,2,1,0:T(8,128)S(1)}, f32[1,1,512,128]{3,2,1,0:T(8,128)S(1)}, u32[]{:S(2)}, u32[]{:S(2)}) collective-permute-start(f32[1,1,512,128]{3,2,1,0:T(8,128)S(1)} %get-tuple-element.112), channel_id=1, source_target_pairs={{0,8},{8,16},{16,24},{24,32},{32,40},{40,48},{48,56},{56,64},{64,7... | collective-permute-start | bytes 786440 | tf_op jit(solution)/shard_map/ppermute | solution.py:24
  70.6 9.1 %collective-permute-start.1 = (f32[1,1,512,128]{3,2,1,0:T(8,128)S(1)}, f32[1,1,512,128]{3,2,1,0:T(8,128)S(1)}, u32[]{:S(2)}, u32[]{:S(2)}) collective-permute-start(f32[1,1,512,128]{3,2,1,0:T(8,128)S(1)} %get-tuple-element.113), channel_id=1, source_target_pairs={{8,0},{16,8},{24,16},{32,24},{40,32},{48,40},{56,48},{64,56},{72,6... | collective-permute-start | bytes 786440 | tf_op jit(solution)/shard_map/ppermute | solution.py:25
  87.0 1.1 copy-start.6
  87.4 4.8 %copy-start.5 = (f32[9,128,128]{2,1,0:T(8,128)S(1)}, f32[9,128,128]{2,1,0:T(8,128)}, u32[]{:S(2)}) copy-start(f32[9,128,128]{2,1,0:T(8,128)} %get-tuple-element.80) | copy-start | bytes 1769476
  88.1 8.2 %copy-start.4 = (f32[9,128,128]{2,1,0:T(8,128)S(1)}, f32[9,128,128]{2,1,0:T(8,128)}, u32[]{:S(2)}) copy-start(f32[9,128,128]{2,1,0:T(8,128)} %get-tuple-element.78) | copy-start | bytes 1769476
  88.1 8.2 %copy-start.7 = (f32[1,1024,128]{2,1,0:T(8,128)S(1)}, f32[1,1024,128]{2,1,0:T(8,128)}, u32[]{:S(2)}) copy-start(f32[1,1024,128]{2,1,0:T(8,128)} %param.21) | copy-start | bytes 1572868
  109.4 17.3 %copy-start.2 = (f32[27,128,128]{2,1,0:T(8,128)S(1)}, f32[27,128,128]{2,1,0:T(8,128)}, u32[]{:S(2)}) copy-start(f32[27,128,128]{2,1,0:T(8,128)} %param.20) | copy-start | bytes 5308420
  157.4 2.0 copy-start.3
  157.4 10.0 %collective-permute-start.2 = (f32[1,1,512,128]{3,2,1,0:T(8,128)S(1)}, f32[1,1,512,128]{3,2,1,0:T(8,128)S(1)}, u32[]{:S(2)}, u32[]{:S(2)}) collective-permute-start(f32[1,1,512,128]{3,2,1,0:T(8,128)S(1)} %get-tuple-element.109), channel_id=1, source_target_pairs={{0,8},{8,16},{16,24},{24,32},{32,40},{40,48},{48,56},{56,64},{64,7... | collective-permute-start | bytes 786440 | tf_op jit(solution)/shard_map/ppermute | solution.py:24
  159.4 9.8 %collective-permute-start.3 = (f32[1,1,512,128]{3,2,1,0:T(8,128)S(1)}, f32[1,1,512,128]{3,2,1,0:T(8,128)S(1)}, u32[]{:S(2)}, u32[]{:S(2)}) collective-permute-start(f32[1,1,512,128]{3,2,1,0:T(8,128)S(1)} %get-tuple-element.108), channel_id=1, source_target_pairs={{8,0},{16,8},{24,16},{32,24},{40,32},{48,40},{56,48},{64,56},{72,6... | collective-permute-start | bytes 786440 | tf_op jit(solution)/shard_map/ppermute | solution.py:25
  165.3 2.1 slice-start
  169.9 233.5 %copy-start.1 = (f32[1,512,128]{2,1,0:T(8,128)S(1)}, f32[1,512,128]{2,1,0:T(8,128)}, u32[]{:S(2)}) copy-start(f32[1,512,128]{2,1,0:T(8,128)} %param.14) | copy-start | bytes 786436
  174.0 227.9 %all-to-all-start.2 = ((f32[64,16,128]{2,1,0:T(8,128)}), f32[64,16,128]{2,1,0:T(8,128)S(1)}, u32[]{:S(2)}, u32[]{:S(2)}) async-start(f32[64,16,128]{2,1,0:T(8,128)} %bitcast.231), calls=%async_computation.2 | async-start | bytes 1048576 | tf_op jit(solution)/shard_map/all_to_all | solution.py:158
  307.6 36.5 %collective-permute-start.10 = (f32[64,128]{1,0:T(8,128)S(1)}, f32[64,128]{1,0:T(8,128)S(1)}, u32[]{:S(2)}, u32[]{:S(2)}) collective-permute-start(f32[64,128]{1,0:T(8,128)S(1)} %fusion), channel_id=1, source_target_pairs={{0,56},{8,64},{16,72},{24,80},{32,88},{40,96},{48,104},{56,112},{6... | collective-permute-start | bytes 98312
  309.5 43.8 %collective-permute-start.11 = (f32[64,128]{1,0:T(8,128)S(1)}, f32[64,128]{1,0:T(8,128)S(1)}, u32[]{:S(2)}, u32[]{:S(2)}) collective-permute-start(f32[64,128]{1,0:T(8,128)S(1)} %fusion), channel_id=1, source_target_pairs={{0,64},{8,72},{16,80},{24,88},{32,96},{40,104},{48,112},{56,120},{... | collective-permute-start | bytes 98312
  314.0 42.5 %collective-permute-start.12 = (f32[64,128]{1,0:T(8,128)S(1)}, f32[64,128]{1,0:T(8,128)S(1)}, u32[]{:S(2)}, u32[]{:S(2)}) collective-permute-start(f32[64,128]{1,0:T(8,128)S(1)} %fusion), channel_id=1, source_target_pairs={{0,72},{8,80},{16,88},{24,96},{32,104},{40,112},{48,120},{56,128},... | collective-permute-start | bytes 98312
  322.4 36.0 %collective-permute-start.4 = (f32[64,128]{1,0:T(8,128)S(1)}, f32[64,128]{1,0:T(8,128)S(1)}, u32[]{:S(2)}, u32[]{:S(2)}) collective-permute-start(f32[64,128]{1,0:T(8,128)S(1)} %fusion), channel_id=1, source_target_pairs={{0,8},{8,16},{16,24},{24,32},{32,40},{40,48},{48,56},{56,64},{64,7... | collective-permute-start | bytes 98312
  324.5 11.8 %collective-permute-start.13 = (f32[54,128]{1,0:T(8,128)S(1)}, f32[54,128]{1,0:T(8,128)S(1)}, u32[]{:S(2)}, u32[]{:S(2)}) collective-permute-start(f32[54,128]{1,0:T(8,128)S(1)} %slice.419), channel_id=1, source_target_pairs={{0,80},{8,88},{16,96},{24,104},{32,112},{40,120},{48,128},{56,136}... | collective-permute-start | bytes 82952
  336.3 27.2 %collective-permute-start.5 = (f32[64,128]{1,0:T(8,128)S(1)}, f32[64,128]{1,0:T(8,128)S(1)}, u32[]{:S(2)}, u32[]{:S(2)}) collective-permute-start(f32[64,128]{1,0:T(8,128)S(1)} %fusion), channel_id=1, source_target_pairs={{0,16},{8,24},{16,32},{24,40},{32,48},{40,56},{48,64},{56,72},{64,... | collective-permute-start | bytes 98312
  344.1 19.4 %collective-permute-start.6 = (f32[64,128]{1,0:T(8,128)S(1)}, f32[64,128]{1,0:T(8,128)S(1)}, u32[]{:S(2)}, u32[]{:S(2)}) collective-permute-start(f32[64,128]{1,0:T(8,128)S(1)} %fusion), channel_id=1, source_target_pairs={{0,24},{8,32},{16,40},{24,48},{32,56},{40,64},{48,72},{56,80},{64,... | collective-permute-start | bytes 98312
  353.4 10.1 %collective-permute-start.7 = (f32[64,128]{1,0:T(8,128)S(1)}, f32[64,128]{1,0:T(8,128)S(1)}, u32[]{:S(2)}, u32[]{:S(2)}) collective-permute-start(f32[64,128]{1,0:T(8,128)S(1)} %fusion), channel_id=1, source_target_pairs={{0,32},{8,40},{16,48},{24,56},{32,64},{40,72},{48,80},{56,88},{64,... | collective-permute-start | bytes 98312
  356.5 9.9 %collective-permute-start.8 = (f32[64,128]{1,0:T(8,128)S(1)}, f32[64,128]{1,0:T(8,128)S(1)}, u32[]{:S(2)}, u32[]{:S(2)}) collective-permute-start(f32[64,128]{1,0:T(8,128)S(1)} %fusion), channel_id=1, source_target_pairs={{0,40},{8,48},{16,56},{24,64},{32,72},{40,80},{48,88},{56,96},{64,... | collective-permute-start | bytes 98312
  358.4 10.8 %collective-permute-start.9 = (f32[64,128]{1,0:T(8,128)S(1)}, f32[64,128]{1,0:T(8,128)S(1)}, u32[]{:S(2)}, u32[]{:S(2)}) collective-permute-start(f32[64,128]{1,0:T(8,128)S(1)} %fusion), channel_id=1, source_target_pairs={{0,48},{8,56},{16,64},{24,72},{32,80},{40,88},{48,96},{56,104},{64... | collective-permute-start | bytes 98312
where the time goes:
time: 411 us; the launch traced here: 404 us
  blocking collectives  154 us (37%)
  starting transfers between devices  102 us (25%)
  matrix products  50.7 us (12%)
  local copies, waits for them, and re-layouts  34.7 us (8%)
  other arithmetic  31.4 us (8%)
  waiting for transfers between devices  24.8 us (6%)
  between operations  6.27 us (2%)
    unnamed x1, blocking collectives  123 us
    unnamed x10, starting transfers between devices  52.3 us
    psum x1, blocking collectives, per_device(): total = lax.psum(share, 'dp')  30.4 us
    dot_general x3, matrix products, per_device(): lax.dot_general(columns, grad_pre, (((0,), (0,)), ((), ())), precision=hi...  25 us
    all_to_all x1, starting transfers between devices, per_device(): lax.all_to_all(send_ids.reshape(slabs, capacity), 'slab', split_axis=0, c...  13.9 us
    dot_general x3, matrix products, per_device(): jnp.dot(columns, group_weight, precision=highest, preferred_element_type=...  13.6 us
    scatter-add x1, other arithmetic, per_device(): grad_visible = jnp.zeros((slots_all * VOX, C), jnp.float32).at[gather_row...  12.2 us
    dot_general x3, matrix products, per_device(): jnp.dot(grad_pre, group_back, precision=highest, preferred_element_type=j...  12.1 us
  transfers between devices with their start and end apart: 17, of which 8 were waited for; matrix products, arithmetic and copies ran while one was open for 35% of the time, Pallas kernels for 0%

commit v1 on v0

--- a/solution.py
+++ b/solution.py
@@ -158,7 +158,9 @@
     came_back = lax.all_to_all(back_points, "slab", split_axis=0, concat_axis=0, tiled=True)
     point_grads = came_back.reshape(slabs * capacity, C)[placement]
     share = lax.psum_scatter(weight_term, "slab", scatter_dimension=0, tiled=True)
-    total = lax.psum(share, "dp")
+    total = share
+    for hop in (1, 2, 4):
+        total = total + lax.ppermute(total, "dp", [(dev, dev ^ hop) for dev in range(8)])
     scale = 1.0 / math.sqrt(windows * slabs * NB * VOX)
     return (activated[None], point_grads[None], total * scale)
 

time: 411 us -> 402 us (0.978)
  the two profiles are of different devices: /device:TPU:4 before, /device:TPU:44 now
where the time goes in v1:
time: 402 us; the launch traced here: 395 us
  blocking collectives  123 us (31%)
  starting transfers between devices  111 us (28%)
  matrix products  50.7 us (13%)
  waiting for transfers between devices  36.9 us (9%)
  local copies, waits for them, and re-layouts  34.8 us (9%)
  other arithmetic  31.3 us (8%)
  between operations  6.29 us (2%)
    unnamed x1, blocking collectives  123 us
    unnamed x10, starting transfers between devices  52.6 us
    dot_general x3, matrix products, per_device(): lax.dot_general(columns, grad_pre, (((0,), (0,)), ((), ())), precision=hi...  25 us
    all_to_all x1, starting transfers between devices, per_device(): lax.all_to_all(send_ids.reshape(slabs, capacity), 'slab', split_axis=0, c...  13.9 us
    ppermute x3, waiting for transfers between devices, per_device(): lax.ppermute(total, 'dp', [(dev, dev ^ hop) for dev in range(8)])  13.7 us
    dot_general x3, matrix products, per_device(): jnp.dot(columns, group_weight, precision=highest, preferred_element_type=...  13.6 us
    scatter-add x1, other arithmetic, per_device(): grad_visible = jnp.zeros((slots_all * VOX, C), jnp.float32).at[gather_row...  12.2 us
    dot_general x3, matrix products, per_device(): jnp.dot(grad_pre, group_back, precision=highest, preferred_element_type=j...  12.1 us
  transfers between devices with their start and end apart: 20, of which 11 were waited for; matrix products, arithmetic and copies ran while one was open for 36% of the time, Pallas kernels for 0%

profile of v1, /device:TPU:44, one launch (start us, length us, event | category | flops | bytes accessed | tf_op | source)
XLA Modules:
  0.0 394.7 jit_solution(10436642978822661147)
XLA Ops:
  8.2 13.9 %all-to-all-start = ((s32[64,1,16]{2,1,0:T(1,128)}), s32[64,1,16]{2,1,0:T(1,128)S(1)}, u32[]{:S(2)}, u32[]{:S(2)}) async-start(s32[64,1,16]{2,1,0:T(1,128)} %bitcast.7), calls=%async_computation | async-start | bytes 65536 | tf_op jit(solution)/shard_map/all_to_all | solution.py:74
  34.9 10.3 %all-to-all-start.1 = ((f32[64,16,128]{2,1,0:T(8,128)}), f32[64,16,128]{2,1,0:T(8,128)S(1)}, u32[]{:S(2)}, u32[]{:S(2)}) async-start(f32[64,16,128]{2,1,0:T(8,128)} %bitcast.10), calls=%async_computation.1 | async-start | bytes 1048576 | tf_op jit(solution)/shard_map/all_to_all | solution.py:71
  46.6 2.9 gather_fusion
  49.8 12.1 %all-to-all-done.1 = f32[64,16,128]{2,1,0:T(8,128)S(1)} async-done(((f32[64,16,128]{2,1,0:T(8,128)}), f32[64,16,128]{2,1,0:T(8,128)S(1)}, u32[]{:S(2)}, u32[]{:S(2)}) %all-to-all-start.1) | async-done | bytes 524320 | tf_op jit(solution)/shard_map/all_to_all | solution.py:71
  61.9 6.2 %scatter_custom_fusion.2 = f32[1025,128]{1,0:T(8,128)S(1)} fusion(s32[1024]{0:T(1024)S(1)} %bitcast.239, f32[1024,128]{1,0:T(8,128)S(1)} %bitcast.232, f32[]{:T(128)} %constant.74.clone.1), kind=kCustom, calls=%fused_computation.81 | custom fusion | flops 131072 | bytes 524804 | tf_op jit(solution)/shard_map/scatter-add | solution.py:83
  70.6 5.2 %collective-permute-start.1 = (f32[1,1,512,128]{3,2,1,0:T(8,128)S(1)}, f32[1,1,512,128]{3,2,1,0:T(8,128)S(1)}, u32[]{:S(2)}, u32[]{:S(2)}) collective-permute-start(f32[1,1,512,128]{3,2,1,0:T(8,128)S(1)} %get-tuple-element.113), channel_id=1, source_target_pairs={{8,0},{16,8},{24,16},{32,24},{40,32},{48,40},{56,48},{64,56},{72,6... | collective-permute-start | bytes 786440 | tf_op jit(solution)/shard_map/ppermute | solution.py:25
  79.9 5.8 %gather_fusion.1 = f32[2000,128]{1,0:T(8,128)S(1)} fusion(f32[2560,128]{1,0:T(8,128)S(1)} %bitcast.213, s32[2048]{0:T(1024)S(1)} %pad_clamp_fusion), kind=kCustom, calls=%fused_computation.1 | custom fusion | bytes 2056000 | tf_op jit(solution)/shard_map/gather | solution.py:100
  88.1 4.1 %fusion.28 = f32[1024,128]{1,0:T(8,128)S(1)} fusion(f32[1024,1152]{1,0:T(8,128)S(1)} %bitcast.221, f32[1152,128]{1,0:T(8,128)S(1)} %bitcast.230), kind=kOutput, calls=%fused_computation.130 | convolution fusion | flops 1811939328 | bytes 5832704 | tf_op jit(solution)/shard_map/dot_general | solution.py:105
  92.2 4.1 %convolution_add_fusion.1 = f32[1024,128]{1,0:T(8,128)S(1)} fusion(f32[1024,128]{1,0:T(8,128)S(1)} %fusion.28, f32[1024,1152]{1,0:T(8,128)S(1)} %bitcast.219, f32[1152,128]{1,0:T(8,128)S(1)} %bitcast.229), kind=kOutput, calls=%fused_computation.12 | convolution fusion | flops 1812070400 | bytes 6356992 | tf_op jit(solution)/shard_map/dot_general | solution.py:105
  96.3 5.4 %fusion.9 = (f32[1024,128]{1,0:T(8,128)S(1)}, f32[1,1024,128]{2,1,0:T(8,128)}) fusion(f32[1,1024,128]{2,1,0:T(8,128)S(1)} %copy-done.7, f32[1024,128]{1,0:T(8,128)S(1)} %convolution_add_fusion.1, f32[1024,1152]{1,0:T(8,128)S(1)} %bitcast.217, f32[1152,128]{1,0:T(8,128)S(1)} %bitcast.228), kind=kOutput, calls=%fused_computation.76 | convolution fusion | flops 1813250048 | bytes 7405568 | tf_op jit(solution)/shard_map/dot_general | solution.py:105
  101.7 7.7 %fusion.29 = f32[1152,128]{1,0:T(8,128)S(1)} fusion(f32[1024,1152]{1,0:T(8,128)S(1)} %bitcast.222, f32[1024,128]{1,0:T(8,128)S(1)} %get-tuple-element.110), kind=kOutput, calls=%fused_computation.131 | convolution fusion | flops 1811939328 | bytes 5832704 | tf_op jit(solution)/shard_map/dot_general | solution.py:116
  109.5 8.7 %fusion.30 = f32[1152,128]{1,0:T(8,128)} fusion(f32[1024,1152]{1,0:T(8,128)S(1)} %bitcast.220, f32[1024,128]{1,0:T(8,128)S(1)} %get-tuple-element.110), kind=kOutput, calls=%fused_computation.132 | convolution fusion | flops 1811939328 | bytes 5832704 | tf_op jit(solution)/shard_map/dot_general | solution.py:116
  118.2 8.5 %fusion.31 = f32[1152,128]{1,0:T(8,128)} fusion(f32[1024,1152]{1,0:T(8,128)S(1)} %bitcast.218, f32[1024,128]{1,0:T(8,128)S(1)} %get-tuple-element.110), kind=kOutput, calls=%fused_computation.133 | convolution fusion | flops 1811939328 | bytes 5832704 | tf_op jit(solution)/shard_map/dot_general | solution.py:116
  126.8 4.2 %fusion.5 = f32[2,8,8,8,9,128]{5,3,2,1,0,4:T(8,128)S(1)} fusion(f32[2,8,8,8,128,1]{4,3,2,1,0,5:T(8,128)S(1)} %bitcast.214, f32[27,128,128]{2,1,0:T(8,128)S(1)} %copy-done.2), kind=kOutput, calls=%fused_computation.17 | convolution fusion | flops 1811939328 | bytes 5832704 | tf_op jit(solution)/shard_map/dot_general | solution.py:126
  131.0 3.8 fusion.3
  134.9 4.0 %fusion.7 = f32[2,8,8,8,9,128]{5,3,4,2,1,0:T(8,128)S(1)} fusion(f32[2,8,8,8,128,1]{4,3,5,2,1,0:T(8,128)S(1)} %bitcast.216, f32[27,128,128]{2,1,0:T(8,128)S(1)} %copy-done.2), kind=kOutput, calls=%fused_computation.19 | convolution fusion | flops 1811939328 | bytes 5832704 | tf_op jit(solution)/shard_map/dot_general | solution.py:126
  141.2 2.9 pad_add_fusion
  145.2 12.2 %scatter_custom_fusion.3 = f32[2560,128]{1,0:T(8,128)S(1)} fusion(s32[2000]{0:T(1024)S(1)} %bitcast.244, f32[2000,128]{1,0:T(8,128)} %reshape.431, f32[]{:T(128)} %constant.74.clone.1), kind=kCustom, calls=%fused_computation.13 | custom fusion | flops 256000 | bytes 1311232 | tf_op jit(solution)/shard_map/scatter-add | solution.py:143
  159.4 5.9 %collective-permute-start.3 = (f32[1,1,512,128]{3,2,1,0:T(8,128)S(1)}, f32[1,1,512,128]{3,2,1,0:T(8,128)S(1)}, u32[]{:S(2)}, u32[]{:S(2)}) collective-permute-start(f32[1,1,512,128]{3,2,1,0:T(8,128)S(1)} %get-tuple-element.108), channel_id=1, source_target_pairs={{8,0},{16,8},{24,16},{32,24},{40,32},{48,40},{56,48},{64,56},{72,6... | collective-permute-start | bytes 786440 | tf_op jit(solution)/shard_map/ppermute | solution.py:25
  169.8 4.0 %gather_fusion.2 = f32[1024,128]{1,0:T(8,128)} fusion(f32[1025,128]{1,0:T(8,128)S(1)} %concatenate.35, s32[1024]{0:T(1024)S(1)} %get-tuple-element.117), kind=kCustom, calls=%fused_computation.2 | custom fusion | bytes 1052672 | tf_op jit(solution)/shard_map/gather | solution.py:157
  173.9 10.3 %all-to-all-start.2 = ((f32[64,16,128]{2,1,0:T(8,128)}), f32[64,16,128]{2,1,0:T(8,128)S(1)}, u32[]{:S(2)}, u32[]{:S(2)}) async-start(f32[64,16,128]{2,1,0:T(8,128)} %bitcast.231), calls=%async_computation.2 | async-start | bytes 1048576 | tf_op jit(solution)/shard_map/all_to_all | solution.py:158
  184.2 123.3 %fusion = f32[64,128]{1,0:T(8,128)S(1)} fusion(f32[3456,128]{1,0:T(8,128)S(1)} %pad_maximum_fusion), kind=kCustom, calls=%all-reduce-scatter | all-reduce-scatter fusion | flops 524289 | bytes 1804288
  311.3 4.7 %collective-permute-start.12 = (f32[64,128]{1,0:T(8,128)S(1)}, f32[64,128]{1,0:T(8,128)S(1)}, u32[]{:S(2)}, u32[]{:S(2)}) collective-permute-start(f32[64,128]{1,0:T(8,128)S(1)} %fusion), channel_id=1, source_target_pairs={{0,48},{8,56},{16,64},{24,72},{32,80},{40,88},{48,96},{56,104},{64... | collective-permute-start | bytes 98312
  316.1 6.1 %collective-permute-start.13 = (f32[64,128]{1,0:T(8,128)S(1)}, f32[64,128]{1,0:T(8,128)S(1)}, u32[]{:S(2)}, u32[]{:S(2)}) collective-permute-start(f32[64,128]{1,0:T(8,128)S(1)} %fusion), channel_id=1, source_target_pairs={{0,56},{8,64},{16,72},{24,80},{32,88},{40,96},{48,104},{56,112},{6... | collective-permute-start | bytes 98312
  322.1 13.3 %collective-permute-start.16 = (f32[54,128]{1,0:T(8,128)S(1)}, f32[54,128]{1,0:T(8,128)S(1)}, u32[]{:S(2)}, u32[]{:S(2)}) collective-permute-start(f32[54,128]{1,0:T(8,128)S(1)} %slice.419), channel_id=1, source_target_pairs={{0,80},{8,88},{16,96},{24,104},{32,112},{40,120},{48,128},{56,136}... | collective-permute-start | bytes 82952
  337.2 14.2 %collective-permute-start.14 = (f32[64,128]{1,0:T(8,128)S(1)}, f32[64,128]{1,0:T(8,128)S(1)}, u32[]{:S(2)}, u32[]{:S(2)}) collective-permute-start(f32[64,128]{1,0:T(8,128)S(1)} %fusion), channel_id=1, source_target_pairs={{0,64},{8,72},{16,80},{24,88},{32,96},{40,104},{48,112},{56,120},{... | collective-permute-start | bytes 98312
  353.4 3.0 collective-permute-start.7
  356.4 3.1 collective-permute-start.8
  364.4 3.3 collective-permute-done.9
  369.4 3.2 collective-permute-start.4
  377.9 4.1 %collective-permute-done.5 = f32[54,128]{1,0:T(8,128)S(1)} collective-permute-done((f32[54,128]{1,0:T(8,128)S(1)}, f32[54,128]{1,0:T(8,128)S(1)}, u32[]{:S(2)}, u32[]{:S(2)}) %collective-permute-start.5) | collective-permute-done | bytes 27680 | tf_op jit(solution)/shard_map/ppermute | solution.py:163
  384.8 7.1 %collective-permute-done.6 = f32[54,128]{1,0:T(8,128)S(1)} collective-permute-done((f32[54,128]{1,0:T(8,128)S(1)}, f32[54,128]{1,0:T(8,128)S(1)}, u32[]{:S(2)}, u32[]{:S(2)}) %collective-permute-start.6) | collective-permute-done | bytes 27680 | tf_op jit(solution)/shard_map/ppermute | solution.py:163
  (106 shorter events, 60.3 us)
Async XLA Ops:
  0.6 31.6 %copy-start = (f32[1,512,128]{2,1,0:T(8,128)S(1)}, f32[1,512,128]{2,1,0:T(8,128)}, u32[]{:S(2)}) copy-start(f32[1,512,128]{2,1,0:T(8,128)} %param.14) | copy-start | bytes 786436
  0.6 45.9 %copy-start.9 = (s32[1000]{0:T(1024)S(1)}, s32[1000]{0:T(1024)}, u32[]{:S(2)}) copy-start(s32[1000]{0:T(1024)} %constant.196) | copy-start | bytes 12004
  0.7 49.0 %copy-start.8 = (s32[1000]{0:T(1024)S(1)}, s32[1000]{0:T(1024)}, u32[]{:S(2)}) copy-start(s32[1000]{0:T(1024)} %constant.90.clone) | copy-start | bytes 12004
  8.2 26.6 %all-to-all-start = ((s32[64,1,16]{2,1,0:T(1,128)}), s32[64,1,16]{2,1,0:T(1,128)S(1)}, u32[]{:S(2)}, u32[]{:S(2)}) async-start(s32[64,1,16]{2,1,0:T(1,128)} %bitcast.7), calls=%async_computation | async-start | bytes 65536 | tf_op jit(solution)/shard_map/all_to_all | solution.py:74
  34.9 27.0 %all-to-all-start.1 = ((f32[64,16,128]{2,1,0:T(8,128)}), f32[64,16,128]{2,1,0:T(8,128)S(1)}, u32[]{:S(2)}, u32[]{:S(2)}) async-start(f32[64,16,128]{2,1,0:T(8,128)} %bitcast.10), calls=%async_computation.1 | async-start | bytes 1048576 | tf_op jit(solution)/shard_map/all_to_all | solution.py:71
  68.2 9.8 %collective-permute-start = (f32[1,1,512,128]{3,2,1,0:T(8,128)S(1)}, f32[1,1,512,128]{3,2,1,0:T(8,128)S(1)}, u32[]{:S(2)}, u32[]{:S(2)}) collective-permute-start(f32[1,1,512,128]{3,2,1,0:T(8,128)S(1)} %get-tuple-element.112), channel_id=1, source_target_pairs={{0,8},{8,16},{16,24},{24,32},{32,40},{40,48},{48,56},{56,64},{64,7... | collective-permute-start | bytes 786440 | tf_op jit(solution)/shard_map/ppermute | solution.py:24
  70.6 9.1 %collective-permute-start.1 = (f32[1,1,512,128]{3,2,1,0:T(8,128)S(1)}, f32[1,1,512,128]{3,2,1,0:T(8,128)S(1)}, u32[]{:S(2)}, u32[]{:S(2)}) collective-permute-start(f32[1,1,512,128]{3,2,1,0:T(8,128)S(1)} %get-tuple-element.113), channel_id=1, source_target_pairs={{8,0},{16,8},{24,16},{32,24},{40,32},{48,40},{56,48},{64,56},{72,6... | collective-permute-start | bytes 786440 | tf_op jit(solution)/shard_map/ppermute | solution.py:25
  87.0 1.1 copy-start.6
  87.4 4.8 %copy-start.5 = (f32[9,128,128]{2,1,0:T(8,128)S(1)}, f32[9,128,128]{2,1,0:T(8,128)}, u32[]{:S(2)}) copy-start(f32[9,128,128]{2,1,0:T(8,128)} %get-tuple-element.80) | copy-start | bytes 1769476
  88.1 8.2 %copy-start.4 = (f32[9,128,128]{2,1,0:T(8,128)S(1)}, f32[9,128,128]{2,1,0:T(8,128)}, u32[]{:S(2)}) copy-start(f32[9,128,128]{2,1,0:T(8,128)} %get-tuple-element.78) | copy-start | bytes 1769476
  88.1 8.2 %copy-start.7 = (f32[1,1024,128]{2,1,0:T(8,128)S(1)}, f32[1,1024,128]{2,1,0:T(8,128)}, u32[]{:S(2)}) copy-start(f32[1,1024,128]{2,1,0:T(8,128)} %param.21) | copy-start | bytes 1572868
  109.5 17.3 %copy-start.2 = (f32[27,128,128]{2,1,0:T(8,128)S(1)}, f32[27,128,128]{2,1,0:T(8,128)}, u32[]{:S(2)}) copy-start(f32[27,128,128]{2,1,0:T(8,128)} %param.20) | copy-start | bytes 5308420
  157.4 2.0 copy-start.3
  157.5 10.0 %collective-permute-start.2 = (f32[1,1,512,128]{3,2,1,0:T(8,128)S(1)}, f32[1,1,512,128]{3,2,1,0:T(8,128)S(1)}, u32[]{:S(2)}, u32[]{:S(2)}) collective-permute-start(f32[1,1,512,128]{3,2,1,0:T(8,128)S(1)} %get-tuple-element.109), channel_id=1, source_target_pairs={{0,8},{8,16},{16,24},{24,32},{32,40},{40,48},{48,56},{56,64},{64,7... | collective-permute-start | bytes 786440 | tf_op jit(solution)/shard_map/ppermute | solution.py:24
  159.4 9.8 %collective-permute-start.3 = (f32[1,1,512,128]{3,2,1,0:T(8,128)S(1)}, f32[1,1,512,128]{3,2,1,0:T(8,128)S(1)}, u32[]{:S(2)}, u32[]{:S(2)}) collective-permute-start(f32[1,1,512,128]{3,2,1,0:T(8,128)S(1)} %get-tuple-element.108), channel_id=1, source_target_pairs={{8,0},{16,8},{24,16},{32,24},{40,32},{48,40},{56,48},{64,56},{72,6... | collective-permute-start | bytes 786440 | tf_op jit(solution)/shard_map/ppermute | solution.py:25
  165.3 2.1 slice-start
  169.8 224.4 %copy-start.1 = (f32[1,512,128]{2,1,0:T(8,128)S(1)}, f32[1,512,128]{2,1,0:T(8,128)}, u32[]{:S(2)}) copy-start(f32[1,512,128]{2,1,0:T(8,128)} %param.14) | copy-start | bytes 786436
  173.9 218.7 %all-to-all-start.2 = ((f32[64,16,128]{2,1,0:T(8,128)}), f32[64,16,128]{2,1,0:T(8,128)S(1)}, u32[]{:S(2)}, u32[]{:S(2)}) async-start(f32[64,16,128]{2,1,0:T(8,128)} %bitcast.231), calls=%async_computation.2 | async-start | bytes 1048576 | tf_op jit(solution)/shard_map/all_to_all | solution.py:158
  307.5 44.0 %collective-permute-start.10 = (f32[64,128]{1,0:T(8,128)S(1)}, f32[64,128]{1,0:T(8,128)S(1)}, u32[]{:S(2)}, u32[]{:S(2)}) collective-permute-start(f32[64,128]{1,0:T(8,128)S(1)} %fusion), channel_id=1, source_target_pairs={{0,32},{8,40},{16,48},{24,56},{32,64},{40,72},{48,80},{56,88},{64,... | collective-permute-start | bytes 98312
  309.4 44.0 %collective-permute-start.11 = (f32[64,128]{1,0:T(8,128)S(1)}, f32[64,128]{1,0:T(8,128)S(1)}, u32[]{:S(2)}, u32[]{:S(2)}) collective-permute-start(f32[64,128]{1,0:T(8,128)S(1)} %fusion), channel_id=1, source_target_pairs={{0,40},{8,48},{16,56},{24,64},{32,72},{40,80},{48,88},{56,96},{64,... | collective-permute-start | bytes 98312
  311.3 45.1 %collective-permute-start.12 = (f32[64,128]{1,0:T(8,128)S(1)}, f32[64,128]{1,0:T(8,128)S(1)}, u32[]{:S(2)}, u32[]{:S(2)}) collective-permute-start(f32[64,128]{1,0:T(8,128)S(1)} %fusion), channel_id=1, source_target_pairs={{0,48},{8,56},{16,64},{24,72},{32,80},{40,88},{48,96},{56,104},{64... | collective-permute-start | bytes 98312
  316.1 43.4 %collective-permute-start.13 = (f32[64,128]{1,0:T(8,128)S(1)}, f32[64,128]{1,0:T(8,128)S(1)}, u32[]{:S(2)}, u32[]{:S(2)}) collective-permute-start(f32[64,128]{1,0:T(8,128)S(1)} %fusion), channel_id=1, source_target_pairs={{0,56},{8,64},{16,72},{24,80},{32,88},{40,96},{48,104},{56,112},{6... | collective-permute-start | bytes 98312
  322.1 15.1 %collective-permute-start.16 = (f32[54,128]{1,0:T(8,128)S(1)}, f32[54,128]{1,0:T(8,128)S(1)}, u32[]{:S(2)}, u32[]{:S(2)}) collective-permute-start(f32[54,128]{1,0:T(8,128)S(1)} %slice.419), channel_id=1, source_target_pairs={{0,80},{8,88},{16,96},{24,104},{32,112},{40,120},{48,128},{56,136}... | collective-permute-start | bytes 82952
  337.2 26.7 %collective-permute-start.14 = (f32[64,128]{1,0:T(8,128)S(1)}, f32[64,128]{1,0:T(8,128)S(1)}, u32[]{:S(2)}, u32[]{:S(2)}) collective-permute-start(f32[64,128]{1,0:T(8,128)S(1)} %fusion), channel_id=1, source_target_pairs={{0,64},{8,72},{16,80},{24,88},{32,96},{40,104},{48,112},{56,120},{... | collective-permute-start | bytes 98312
  351.5 12.5 %collective-permute-start.15 = (f32[64,128]{1,0:T(8,128)S(1)}, f32[64,128]{1,0:T(8,128)S(1)}, u32[]{:S(2)}, u32[]{:S(2)}) collective-permute-start(f32[64,128]{1,0:T(8,128)S(1)} %fusion), channel_id=1, source_target_pairs={{0,72},{8,80},{16,88},{24,96},{32,104},{40,112},{48,120},{56,128},... | collective-permute-start | bytes 98312
  353.4 10.6 %collective-permute-start.7 = (f32[64,128]{1,0:T(8,128)S(1)}, f32[64,128]{1,0:T(8,128)S(1)}, u32[]{:S(2)}, u32[]{:S(2)}) collective-permute-start(f32[64,128]{1,0:T(8,128)S(1)} %fusion), channel_id=1, source_target_pairs={{0,8},{8,16},{16,24},{24,32},{32,40},{40,48},{48,56},{56,64},{64,7... | collective-permute-start | bytes 98312
  356.4 8.0 %collective-permute-start.8 = (f32[64,128]{1,0:T(8,128)S(1)}, f32[64,128]{1,0:T(8,128)S(1)}, u32[]{:S(2)}, u32[]{:S(2)}) collective-permute-start(f32[64,128]{1,0:T(8,128)S(1)} %fusion), channel_id=1, source_target_pairs={{0,16},{8,24},{16,32},{24,40},{32,48},{40,56},{48,64},{56,72},{64,... | collective-permute-start | bytes 98312
  359.5 8.3 %collective-permute-start.9 = (f32[64,128]{1,0:T(8,128)S(1)}, f32[64,128]{1,0:T(8,128)S(1)}, u32[]{:S(2)}, u32[]{:S(2)}) collective-permute-start(f32[64,128]{1,0:T(8,128)S(1)} %fusion), channel_id=1, source_target_pairs={{0,24},{8,32},{16,40},{24,48},{32,56},{40,64},{48,72},{56,80},{64,... | collective-permute-start | bytes 98312
  369.4 5.8 %collective-permute-start.4 = (f32[54,128]{1,0:T(8,128)S(1)}, f32[54,128]{1,0:T(8,128)S(1)}, u32[]{:S(2)}, u32[]{:S(2)}) collective-permute-start(f32[54,128]{1,0:T(8,128)S(1)} %constant_dynamic-slice_fusion), channel_id=1, source_target_pairs={{0,1},{1,0},{2,3},{3,2},{4,5},{5,4},{6,7},{7,6},{8,9},{9,8},{10,11... | collective-permute-start | bytes 82952 | tf_op jit(solution)/shard_map/ppermute | solution.py:163
  375.2 6.8 %collective-permute-start.5 = (f32[54,128]{1,0:T(8,128)S(1)}, f32[54,128]{1,0:T(8,128)S(1)}, u32[]{:S(2)}, u32[]{:S(2)}) collective-permute-start(f32[54,128]{1,0:T(8,128)S(1)} %fusion.47), channel_id=1, source_target_pairs={{0,2},{1,3},{2,0},{3,1},{4,6},{5,7},{6,4},{7,5},{8,10},{9,11},{10,... | collective-permute-start | bytes 82952 | tf_op jit(solution)/shard_map/ppermute | solution.py:163
  382.0 10.0 %collective-permute-start.6 = (f32[54,128]{1,0:T(8,128)S(1)}, f32[54,128]{1,0:T(8,128)S(1)}, u32[]{:S(2)}, u32[]{:S(2)}) collective-permute-start(f32[54,128]{1,0:T(8,128)S(1)} %add.335), channel_id=1, source_target_pairs={{0,4},{1,5},{2,6},{3,7},{4,0},{5,1},{6,2},{7,3},{8,12},{9,13},{10,... | collective-permute-start | bytes 82952 | tf_op jit(solution)/shard_map/ppermute | solution.py:163
